TPU v7x, 32 devices: a whole 2x2x4 slice. The times are simulated.
32 devices in a mesh: section: 2 (over x), replica: 16 (over z, y, core).
Axes of the slice: x: 2, y: 2, z: 4, core: 2. Of those that a mesh axis runs over, the one named last changes fastest.
Arguments:
- pending_section_entries: bfloat16 [2, 32, 14, 14, 512], P('section', 'replica'), may hold values from -40 to 40
- arriving_microsets: bfloat16 [1, 32, 14, 14, 512], P(None, 'replica'), may hold values from -40 to 40
- opening_filter_kernel: bfloat16 [2, 3, 3, 512, 512], P('section'), may hold values from -0.09375 to 0.09375
- closing_filter_kernel: bfloat16 [2, 3, 3, 512, 512], P('section'), may hold values from -0.09375 to 0.09375
- stretch_factors: float32 [2, 2, 512], P('section'), may hold values from 0.5 to 1.5
- shift_terms: float32 [2, 2, 512], P('section'), may hold values from -3 to 3
Outputs:
- produced: bfloat16 [2, 2, 32, 14, 14, 512], P('section', None, 'replica')
All inputs are finite; a program needn't handle non-finite values.
Results may differ from a plain program's by a relative error of at most 0.0084.
Values may be sent and summed in bfloat16 or wider, within the bound.
A program may use at most 64 MiB of HBM per device.

v0:
```python
import jax
import jax.numpy as jnp
from jax import lax
from jax.sharding import PartitionSpec as P

TICKS = 2


def from_behind(shard, axis, by):
    length = lax.axis_size(axis)
    pairs = [(i, i + by) for i in range(length) if 0 <= i + by < length]
    return lax.ppermute(shard, axis, pairs)


def convolve(maps, kernel):
    return lax.conv_general_dilated(
        maps,
        kernel,
        (1, 1),
        "SAME",
        dimension_numbers=("NHWC", "HWIO", "NHWC"),
        preferred_element_type=jnp.float32,
    )


def batch_statistics(conv_out, replica_total):
    summed = lax.psum(jnp.sum(conv_out, axis=(0, 1, 2)), "replica")
    mean = summed / replica_total
    centred = conv_out - mean
    spread = lax.psum(jnp.sum(centred * centred, axis=(0, 1, 2)), "replica")
    var = spread / replica_total
    return (mean, var)


def coefficients(conv_out, gain, bias, replica_total):
    mean, var = batch_statistics(conv_out, replica_total)
    scale = gain * lax.rsqrt(var + 1e-05)
    return (scale, bias - mean * scale)


def store(conv_out):
    return lax.optimization_barrier(conv_out.astype(jnp.bfloat16))


def normalize(stored, scale, offset):
    return jnp.maximum(stored.astype(jnp.float32) * scale + offset, 0.0).astype(jnp.bfloat16)


def body(
    pending_section_entries,
    arriving_microsets,
    opening_filter_kernel,
    closing_filter_kernel,
    stretch_factors,
    shift_terms,
):
    replica_total = (
        lax.axis_size("replica")
        * pending_section_entries.shape[1]
        * pending_section_entries.shape[2]
        * pending_section_entries.shape[3]
    )
    is_first = lax.axis_index("section") == 0
    first_kernel = opening_filter_kernel[0]
    second_kernel = closing_filter_kernel[0]
    current_feature_map = pending_section_entries[0]
    results = []
    for tick in range(TICKS):
        conv_one = convolve(current_feature_map, first_kernel)
        scale_one, offset_one = coefficients(
            conv_one, stretch_factors[0, 0], shift_terms[0, 0], replica_total
        )
        hidden = normalize(store(conv_one), scale_one, offset_one)
        conv_two = convolve(hidden, second_kernel)
        stored_two = store(conv_two)
        last = tick + 1 == TICKS
        scale_two, offset_two = coefficients(
            conv_two, stretch_factors[0, 1], shift_terms[0, 1], replica_total
        )
        output = normalize(stored_two, scale_two, offset_two)
        if not last:
            moved = from_behind(output, "section", 1)
        results.append(output)
        if not last:
            current_feature_map = jnp.where(is_first, arriving_microsets[tick], moved)
    return jnp.stack(results, axis=0)[None]


def solution(mesh):
    in_specs = (
        P("section", "replica", None, None, None),
        P(None, "replica", None, None, None),
        P("section", None, None, None, None),
        P("section", None, None, None, None),
        P("section", None, None),
        P("section", None, None),
    )
    out_specs = P("section", None, "replica", None, None, None)
    return jax.shard_map(body, mesh=mesh, in_specs=in_specs, out_specs=out_specs, check_vma=False)
```

profile of v0, /device:TPU:3, one launch (start us, length us, event | category | flops | bytes accessed | tf_op | source)
XLA Modules:
  0.0 283.8 jit_solution(8439790721136657409)
XLA Ops:
  0.0 0.0 copy-start.1
  0.0 0.8 fusion.68
  0.8 0.8 fusion.69
  1.5 1.4 pad
  3.0 0.1 copy.16
  3.1 0.1 slice.28
  3.2 0.0 copy-done.1
  3.2 4.6 %select_reduce_fusion.7 = (f32[512]{0:T(512)S(1)}, f32[14,16,2,512]{3,1,2,0:T(8,128)S(1)}) fusion(pred[16,2]{0,1:T(4,128)(4,1)S(1)} %copy-done.1, bf16[1,3,3,512,512]{4,3,2,1,0:T(8,128)(2,1)} %param.8, bf16[14,2,7,2,512]{4,2,1,3,0:T(8,128)(2,1)S(1)} %slice.28, bf16[14,2,8,2,512]{4,2,1,3,0:T(8,128)(2,1)S(1)} %copy.16), kind=kOutput, calls=%fused_computation.45 | convolution fusion | flops 2016706048 | bytes 6498336 | tf_op jit(solution)/shard_map/conv_general_dilated | solution.py:16
  7.8 29.8 %psum.56 = f32[512]{0:T(512)S(1)} all-reduce(f32[512]{0:T(512)S(1)} %get-tuple-element.25), channel_id=1, replica_groups=mesh['section'=2,'replica'=16] {'replica'}, use_global_device_ids=true, to_apply=%region_1.0 | all-reduce | flops 512 | bytes 4096 | tf_op jit(solution)/shard_map/psum | solution.py:27
  37.6 0.2 select_reduce_fusion.6
  37.8 33.2 %psum.57 = f32[512]{0:T(512)S(1)} all-reduce(f32[512]{0:T(512)S(1)} %get-tuple-element.19), channel_id=1, replica_groups=mesh['section'=2,'replica'=16] {'replica'}, use_global_device_ids=true, to_apply=%region_3.0 | all-reduce | flops 512 | bytes 4096 | tf_op jit(solution)/shard_map/psum | solution.py:30
  71.1 0.5 copy.17
  71.6 0.2 reshape.18
  71.8 0.1 fusion.48
  71.9 0.1 pad.2
  72.1 0.2 reshape.23
  72.3 0.1 copy.19
  72.3 0.1 slice.30
  72.5 4.6 %select_reduce_fusion.5 = (f32[512]{0:T(512)S(1)}, f32[14,16,2,512]{3,1,2,0:T(8,128)S(1)}) fusion(pred[16,2]{0,1:T(4,128)(4,1)S(1)} %copy-done.1, bf16[1,3,3,512,512]{4,3,2,1,0:T(8,128)(2,1)} %param.9, bf16[14,2,7,2,512]{4,2,1,3,0:T(8,128)(2,1)S(1)} %slice.30, bf16[14,2,8,2,512]{4,2,1,3,0:T(8,128)(2,1)S(1)} %copy.19), kind=kOutput, calls=%fused_computation.43 | convolution fusion | flops 2016706048 | bytes 6498336 | tf_op jit(solution)/shard_map/conv_general_dilated | solution.py:16
  77.1 29.5 %psum.58 = f32[512]{0:T(512)S(1)} all-reduce(f32[512]{0:T(512)S(1)} %get-tuple-element.27), channel_id=1, replica_groups=mesh['section'=2,'replica'=16] {'replica'}, use_global_device_ids=true, to_apply=%region_5.0 | all-reduce | flops 512 | bytes 4096 | tf_op jit(solution)/shard_map/psum | solution.py:27
  106.6 0.2 select_reduce_fusion.4
  106.8 29.5 %psum.59 = f32[512]{0:T(512)S(1)} all-reduce(f32[512]{0:T(512)S(1)} %get-tuple-element.17), channel_id=1, replica_groups=mesh['section'=2,'replica'=16] {'replica'}, use_global_device_ids=true, to_apply=%region_7.0 | all-reduce | flops 512 | bytes 4096 | tf_op jit(solution)/shard_map/psum | solution.py:30
  136.3 0.5 copy.20
  136.8 0.0 copy-start
  136.8 0.2 reshape.27
  137.1 0.1 maximum_convert_fusion.2
  137.2 1.3 collective-permute-start
  138.5 0.1 fusion.70
  138.7 11.9 %collective-permute-done = bf16[2,14,14,512]{3,2,0,1:T(8,128)(2,1)S(1)} collective-permute-done((bf16[2,14,14,512]{3,2,0,1:T(8,128)(2,1)S(1)}, bf16[2,14,14,512]{3,2,0,1:T(8,128)(2,1)S(1)}, u32[]{:S(2)}, u32[]{:S(2)}) %collective-permute-start) | collective-permute-done | bytes 401440 | tf_op jit(solution)/shard_map/ppermute | solution.py:12
  150.5 0.0 copy-done
  150.5 0.1 fusion.55
  150.6 0.1 pad.4
  150.7 0.2 reshape.32
  150.9 0.1 copy.23
  151.0 0.1 slice.32
  151.1 4.6 %select_reduce_fusion.3 = (f32[512]{0:T(512)S(1)}, f32[14,16,2,512]{3,1,2,0:T(8,128)S(1)}) fusion(pred[16,2]{0,1:T(4,128)(4,1)S(1)} %copy-done.1, bf16[1,3,3,512,512]{4,3,2,1,0:T(8,128)(2,1)} %param.8, bf16[14,2,7,2,512]{4,2,1,3,0:T(8,128)(2,1)S(1)} %slice.32, bf16[14,2,8,2,512]{4,2,1,3,0:T(8,128)(2,1)S(1)} %copy.23), kind=kOutput, calls=%fused_computation.41 | convolution fusion | flops 2016706048 | bytes 6498336 | tf_op jit(solution)/shard_map/conv_general_dilated | solution.py:16
  155.7 30.4 %psum.60 = f32[512]{0:T(512)S(1)} all-reduce(f32[512]{0:T(512)S(1)} %get-tuple-element.29), channel_id=1, replica_groups=mesh['section'=2,'replica'=16] {'replica'}, use_global_device_ids=true, to_apply=%region_9.10 | all-reduce | flops 512 | bytes 4096 | tf_op jit(solution)/shard_map/psum | solution.py:27
  186.1 0.2 select_reduce_fusion.2
  186.3 29.5 %psum.61 = f32[512]{0:T(512)S(1)} all-reduce(f32[512]{0:T(512)S(1)} %get-tuple-element.15), channel_id=1, replica_groups=mesh['section'=2,'replica'=16] {'replica'}, use_global_device_ids=true, to_apply=%region_11.12 | all-reduce | flops 512 | bytes 4096 | tf_op jit(solution)/shard_map/psum | solution.py:30
  215.8 0.5 copy.24
  216.3 0.2 reshape.36
  216.5 0.1 fusion.49
  216.7 0.1 pad.6
  216.8 0.2 reshape.41
  217.0 0.1 copy.26
  217.1 0.1 slice.34
  217.2 4.6 %select_reduce_fusion.1 = (f32[512]{0:T(512)S(1)}, f32[14,16,2,512]{3,1,2,0:T(8,128)S(1)}) fusion(pred[16,2]{0,1:T(4,128)(4,1)S(1)} %copy-done.1, bf16[1,3,3,512,512]{4,3,2,1,0:T(8,128)(2,1)} %param.9, bf16[14,2,7,2,512]{4,2,1,3,0:T(8,128)(2,1)S(1)} %slice.34, bf16[14,2,8,2,512]{4,2,1,3,0:T(8,128)(2,1)S(1)} %copy.26), kind=kOutput, calls=%fused_computation.39 | convolution fusion | flops 2016706048 | bytes 6498336 | tf_op jit(solution)/shard_map/conv_general_dilated | solution.py:16
  221.8 29.5 %psum.62 = f32[512]{0:T(512)S(1)} all-reduce(f32[512]{0:T(512)S(1)} %get-tuple-element.31), channel_id=1, replica_groups=mesh['section'=2,'replica'=16] {'replica'}, use_global_device_ids=true, to_apply=%region_13.14 | all-reduce | flops 512 | bytes 4096 | tf_op jit(solution)/shard_map/psum | solution.py:27
  251.3 0.2 select_reduce_fusion
  251.6 29.5 %psum.63 = f32[512]{0:T(512)S(1)} all-reduce(f32[512]{0:T(512)S(1)} %get-tuple-element.13), channel_id=1, replica_groups=mesh['section'=2,'replica'=16] {'replica'}, use_global_device_ids=true, to_apply=%region_15.16 | all-reduce | flops 512 | bytes 4096 | tf_op jit(solution)/shard_map/psum | solution.py:30
  281.1 0.5 copy.27
  281.6 0.2 reshape.45
  281.8 0.1 fusion.50
  281.9 0.1 maximum_bitcast_fusion
  282.1 1.7 copy.28
  (12 shorter events, 0.2 us)
Async XLA Ops:
  0.0 3.2 %copy-start.1 = (pred[16,2]{0,1:T(4,128)(4,1)S(1)}, pred[16,2]{0,1:T(4,128)(4,1)}, u32[]{:S(2)}) copy-start(pred[16,2]{0,1:T(4,128)(4,1)} %constant.53) | copy-start | bytes 100
  136.8 13.7 %copy-start = (bf16[1,2,14,14,512]{4,1,3,2,0:T(2,128)(2,1)S(1)}, bf16[1,2,14,14,512]{4,1,3,2,0:T(2,128)(2,1)}, u32[]{:S(2)}) copy-start(bf16[1,2,14,14,512]{4,1,3,2,0:T(2,128)(2,1)} %param.7) | copy-start | bytes 1204228
  137.2 13.3 %collective-permute-start = (bf16[2,14,14,512]{3,2,0,1:T(8,128)(2,1)S(1)}, bf16[2,14,14,512]{3,2,0,1:T(8,128)(2,1)S(1)}, u32[]{:S(2)}, u32[]{:S(2)}) collective-permute-start(bf16[2,14,14,512]{3,2,0,1:T(8,128)(2,1)S(1)} %maximum_convert_fusion.2), channel_id=1, source_target_pairs={{0,16},{1,17},{2,18},{3,19},{4,20},{5,21},{6,22},{7,23},{8,24},{9,... | collective-permute-start | bytes 1204232 | tf_op jit(solution)/shard_map/ppermute | solution.py:12
where the time goes:
time: 285 us; the launch traced here: 284 us
  blocking collectives  241 us (85%)
  matrix products  18.6 us (7%)
  waiting for transfers between devices  11.9 us (4%)
  local copies, waits for them, and re-layouts  9.1 us (3%)
    psum x4, blocking collectives, batch_statistics(): spread = lax.psum(jnp.sum(centred * centred, axis=(0, 1, 2)), 'replica')  122 us
    psum x4, blocking collectives, batch_statistics(): summed = lax.psum(jnp.sum(conv_out, axis=(0, 1, 2)), 'replica')  119 us
    conv_general_dilated x4, matrix products, convolve(): lax.conv_general_dilated(maps, kernel, (1, 1), 'SAME', dimension_numbers=...  18.6 us
    ppermute x1, waiting for transfers between devices, from_behind(): return lax.ppermute(shard, axis, pairs)  11.9 us
  transfers between devices with their start and end apart: 1, of which 1 were waited for; matrix products, arithmetic and copies ran while one was open for 0% of the time, Pallas kernels for 0%

commit v1 on v0

v1 whole, which is shorter than its diff:
```python
import functools

import jax
import jax.numpy as jnp
from jax import lax
from jax.experimental import pallas as pl
from jax.experimental.pallas import tpu as pltpu
from jax.sharding import PartitionSpec as P

MESH = pl.DeviceIdType.MESH
F32 = jnp.float32
BF16 = jnp.bfloat16
LANES = 128
PITCH = 16
TILE = 256


def kernel(
    sections,
    replicas,
    pend,
    arriving,
    first,
    second,
    gain,
    bias,
    out,
    maps,
    weights,
    taps,
    y,
    sent,
    landed,
    mine,
    slots,
    coef,
    moved_coef,
    affine,
    result,
    map_sem,
    weight_sem,
    out_sem,
    stat_send,
    stat_recv,
    bulk_send,
    bulk_recv,
    coef_send,
    coef_recv,
):
    images, rows, cols, channels = maps.shape[1:]
    chunks = channels // LANES
    halves = channels // TILE
    blocks = y.shape[0]
    cells = images * rows * cols
    sec = lax.axis_index("section")
    me = lax.axis_index("replica")

    barrier = pltpu.get_barrier_semaphore()

    def greet(d, carry):
        peer = lax.rem(me + d, replicas)
        pl.semaphore_signal(
            barrier, inc=1, device_id={"section": sec, "replica": peer}, device_id_type=MESH
        )
        return carry

    lax.fori_loop(1, replicas, greet, 0)

    @pl.when(sec > 0)
    def _():
        pl.semaphore_signal(
            barrier, inc=1, device_id={"section": sec - 1, "replica": me}, device_id_type=MESH
        )

    @pl.when(sec < sections - 1)
    def _():
        pl.semaphore_signal(
            barrier, inc=1, device_id={"section": sec + 1, "replica": me}, device_id_type=MESH
        )

    map_copies = [
        pltpu.make_async_copy(pend.at[0], maps.at[0], map_sem.at[0]),
        pltpu.make_async_copy(arriving.at[0], maps.at[1], map_sem.at[1]),
    ]
    weight_copies = [
        [
            pltpu.make_async_copy(src.at[0, dy], weights.at[layer, dy], weight_sem.at[layer, dy])
            for dy in range(3)
        ]
        for layer, src in enumerate((first, second))
    ]
    map_copies[0].start()
    for layer in range(2):
        for dy in range(3):
            weight_copies[layer][dy].start()
    map_copies[1].start()

    for layer in range(2):
        for k in range(chunks):
            lane = slice(k * LANES, (k + 1) * LANES)
            affine[layer, k : k + 1, :] = gain[0, layer : layer + 1, lane]
            affine[layer, chunks + k : chunks + k + 1, :] = bias[0, layer : layer + 1, lane]

    pad = jnp.zeros((halves, PITCH, 3 * TILE), BF16)
    for i in range(images + 1):
        at = i * (rows + 1) * PITCH
        taps[:, at : at + PITCH, :] = pad

    inside = lax.broadcasted_iota(jnp.int32, (rows, PITCH, LANES), 1) < cols

    def lay(i, k, values):
        flat = jnp.where(inside, values, 0.0).reshape(rows * PITCH, LANES)
        at = (i * (rows + 1) + 1) * PITCH
        half, lane = (k * LANES) // TILE, (k * LANES) % TILE
        where = slice(at, at + rows * PITCH)
        taps[half, where, lane : lane + LANES] = pltpu.roll(flat, 1, 0).astype(BF16)
        taps[half, where, TILE + lane : TILE + lane + LANES] = flat.astype(BF16)
        taps[half, where, 2 * TILE + lane : 2 * TILE + lane + LANES] = pltpu.roll(
            flat, rows * PITCH - 1, 0
        ).astype(BF16)

    def block_rows(i):
        return slice(i * (rows + 1), i * (rows + 1) + rows)

    def lay_maps(which):
        for i in range(images):
            for k in range(chunks):
                lane = slice(k * LANES, (k + 1) * LANES)
                y[block_rows(i), 0:cols, lane] = maps[which, i, :, :, lane].astype(F32)
                lay(i, k, y[block_rows(i), :, lane])

    def multiply(layer, n, parts, add):
        lane = slice(n * TILE, (n + 1) * TILE)
        total = None
        for dy, half in parts:
            left = taps[half, dy * PITCH : (dy + blocks) * PITCH, :]
            right = weights[layer, dy, :, half * TILE : (half + 1) * TILE, lane]
            term = jnp.dot(left, right.reshape(3 * TILE, TILE), preferred_element_type=F32)
            total = term if total is None else total + term
        total = total.reshape(blocks, PITCH, TILE)
        y[:, :, lane] = y[:, :, lane] + total if add else total

    every = [(dy, half) for half in range(halves) for dy in range(3)]

    def gather_statistics(phase):
        for k in range(chunks):
            lane = slice(k * LANES, (k + 1) * LANES)
            total = 0.0
            for i in range(images):
                total = total + jnp.sum(jnp.where(inside, y[block_rows(i), :, lane], 0.0), axis=0)
            mean = jnp.sum(total, axis=0, keepdims=True) / cells
            spread = 0.0
            for i in range(images):
                centred = jnp.where(inside, y[block_rows(i), :, lane] - mean, 0.0)
                spread = spread + jnp.sum(centred * centred, axis=0)
            mine[phase, k : k + 1, :] = mean
            mine[phase, chunks + k : chunks + k + 1, :] = jnp.sum(spread, axis=0, keepdims=True)

    def send_statistics(phase):
        def send(d, carry):
            peer = lax.rem(me + d, replicas)
            pltpu.make_async_remote_copy(
                src_ref=mine.at[phase],
                dst_ref=slots.at[phase, d - 1],
                send_sem=stat_send.at[phase],
                recv_sem=stat_recv.at[phase],
                device_id={"section": sec, "replica": peer},
                device_id_type=MESH,
            ).start()
            return carry

        lax.fori_loop(1, replicas, send, 0)

    def combine(phase, layer):
        pltpu.make_async_copy(slots.at[phase], slots.at[phase], stat_recv.at[phase]).wait()
        own = mine[phase]
        others = slots[phase]
        total = own + jnp.sum(others, axis=0)
        mean = total[0:chunks] / replicas
        apart = (own[0:chunks] - mean) ** 2 + jnp.sum(
            (others[:, 0:chunks] - mean[None]) ** 2, axis=0
        )
        var = (total[chunks:] + apart * cells) / (cells * replicas)
        scale = affine[layer, 0:chunks, :] * lax.rsqrt(var + 1e-05)
        coef[phase, 0:chunks, :] = scale
        coef[phase, chunks:, :] = affine[layer, chunks:, :] - mean * scale

    def activate(values, table, k):
        scale = table[k : k + 1, :]
        offset = table[chunks + k : chunks + k + 1, :]
        return jnp.maximum(values * scale[None] + offset[None], 0.0)

    def lay_hidden(phase):
        table = coef[phase]
        for k in range(chunks):
            lane = slice(k * LANES, (k + 1) * LANES)
            for i in range(images):
                lay(i, k, activate(y[block_rows(i), :, lane], table, k))

    def give_result(tick, phase):
        table = coef[phase]
        for k in range(chunks):
            lane = slice(k * LANES, (k + 1) * LANES)
            for i in range(images):
                done = activate(y[block_rows(i), 0:cols, lane], table, k)
                result[tick, i, :, :, lane] = done.astype(BF16)
        pltpu.make_async_copy(result.at[tick], out.at[0, tick], out_sem.at[tick]).start()

    map_copies[0].wait()
    lay_maps(0)
    for dy in range(3):
        weight_copies[0][dy].wait()
        for n in range(halves):
            multiply(0, n, [(dy, half) for half in range(halves)], dy > 0)
    gather_statistics(0)
    pl.semaphore_wait(
        barrier,
        replicas - 1 + (sec > 0).astype(jnp.int32) + (sec < sections - 1).astype(jnp.int32),
    )
    send_statistics(0)
    for dy in range(3):
        weight_copies[1][dy].wait()
    map_copies[1].wait()
    combine(0, 0)
    lay_hidden(0)

    def bulk(n):
        return pltpu.make_async_remote_copy(
            src_ref=sent.at[n],
            dst_ref=landed.at[n],
            send_sem=bulk_send.at[n],
            recv_sem=bulk_recv.at[n],
            device_id={"section": sec + 1, "replica": me},
            device_id_type=MESH,
        )

    def coefficients():
        return pltpu.make_async_remote_copy(
            src_ref=coef.at[1],
            dst_ref=moved_coef,
            send_sem=coef_send,
            recv_sem=coef_recv,
            device_id={"section": sec + 1, "replica": me},
            device_id_type=MESH,
        )

    for n in range(halves):
        multiply(1, n, every, False)
        lane = slice(n * TILE, (n + 1) * TILE)
        for i in range(images):
            sent[n, i] = y[block_rows(i), :, lane].astype(BF16)

        @pl.when(sec < sections - 1)
        def _():
            bulk(n).start()

    gather_statistics(1)
    send_statistics(1)
    combine(1, 1)

    @pl.when(sec < sections - 1)
    def _():
        coefficients().start()

    give_result(0, 1)

    @pl.when(sec == 0)
    def _():
        lay_maps(1)

    def lay_landed(half):
        bulk(half).wait_recv()
        table = moved_coef[...]
        for k in range(half * TILE // LANES, (half + 1) * TILE // LANES):
            at = k * LANES - half * TILE
            for i in range(images):
                values = landed[half, i, :, :, at : at + LANES].astype(F32)
                lay(i, k, activate(values, table, k))

    for half in range(halves):

        @pl.when(sec > 0)
        def _():
            if half == 0:
                coefficients().wait_recv()
            lay_landed(half)

        for n in range(halves):
            multiply(0, n, [(dy, half) for dy in range(3)], half > 0)
    gather_statistics(2)
    send_statistics(2)
    combine(2, 0)
    lay_hidden(2)

    for n in range(halves):
        multiply(1, n, every, False)
    gather_statistics(3)
    send_statistics(3)
    combine(3, 1)
    give_result(1, 3)

    for phase in range(4):
        pltpu.make_async_copy(slots.at[phase], slots.at[phase], stat_send.at[phase]).wait()

    @pl.when(sec < sections - 1)
    def _():
        for n in range(halves):
            bulk(n).wait_send()
        coefficients().wait_send()

    for tick in range(2):
        pltpu.make_async_copy(result.at[tick], out.at[0, tick], out_sem.at[tick]).wait()


def solution(mesh):
    sections, replicas = mesh.shape["section"], mesh.shape["replica"]

    def body(pend, arriving, first, second, gain, bias):
        images, rows, cols, channels = pend.shape[1:]
        blocks = images * (rows + 1) - 1
        halves = channels // TILE
        tile = 2 * channels // LANES
        dma = pltpu.SemaphoreType.DMA
        anywhere = pl.BlockSpec(memory_space=pl.ANY)
        vmem = pl.BlockSpec(memory_space=pltpu.VMEM)
        depth = 9 * channels * channels
        return pl.pallas_call(
            functools.partial(kernel, sections, replicas),
            out_shape=jax.ShapeDtypeStruct((1, 2, images, rows, cols, channels), BF16),
            in_specs=[anywhere] * 4 + [vmem] * 2,
            out_specs=anywhere,
            scratch_shapes=[
                pltpu.VMEM((2, images, rows, cols, channels), BF16),
                pltpu.VMEM((2, 3, 3, channels, channels), BF16),
                pltpu.VMEM((halves, (blocks + 2) * PITCH, 3 * TILE), BF16),
                pltpu.VMEM((blocks, PITCH, channels), F32),
                pltpu.VMEM((halves, images, rows, PITCH, TILE), BF16),
                pltpu.VMEM((halves, images, rows, PITCH, TILE), BF16),
                pltpu.VMEM((4, tile, LANES), F32),
                pltpu.VMEM((4, replicas - 1, tile, LANES), F32),
                pltpu.VMEM((4, tile, LANES), F32),
                pltpu.VMEM((tile, LANES), F32),
                pltpu.VMEM((2, tile, LANES), F32),
                pltpu.VMEM((2, images, rows, cols, channels), BF16),
                dma((2,)),
                dma((2, 3)),
                dma((2,)),
                dma((4,)),
                dma((4,)),
                dma((halves,)),
                dma((halves,)),
                dma,
                dma,
            ],
            compiler_params=pltpu.CompilerParams(
                collective_id=0, has_side_effects=True, vmem_limit_bytes=56 * 2**20
            ),
            cost_estimate=pl.CostEstimate(
                flops=8 * images * rows * cols * depth,
                bytes_accessed=4 * depth,
                transcendentals=0,
            ),
            name="relay",
        )(pend, arriving, first, second, gain, bias)

    in_specs = (
        P("section", "replica", None, None, None),
        P(None, "replica", None, None, None),
        P("section", None, None, None, None),
        P("section", None, None, None, None),
        P("section", None, None),
        P("section", None, None),
    )
    out_specs = P("section", None, "replica", None, None, None)
    return jax.shard_map(body, mesh=mesh, in_specs=in_specs, out_specs=out_specs, check_vma=False)
```

time: 285 us -> 48.8 us (0.17)
  blocking collectives: 241 us -> 0 us
  Pallas kernels: 0 us -> 42 us
  matrix products: 18.6 us -> 0 us
  waiting for transfers between devices: 11.9 us -> 0 us
    psum x8 -> x0, blocking collectives: 241 us -> none  [the longest x4 122 us: batch_statistics(): spread = lax.psum(jnp.sum(centred * centred, axis=(0, 1, 2)), 'replica')]
    pallas_call x0 -> x1, Pallas kernels: none -> 42 us  [body(): pl.pallas_call(functools.partial(kernel, sections, replicas), out_shape=j...]
    conv_general_dilated x4 -> x0, matrix products: 18.6 us -> none  [convolve(): lax.conv_general_dilated(maps, kernel, (1, 1), 'SAME', dimension_numbers=...]
    ppermute x1 -> x0, waiting for transfers between devices: 11.9 us -> none  [from_behind(): return lax.ppermute(shard, axis, pairs)]
    unnamed x4 -> x2, local copies, waits for them, and re-layouts: 0.01 us -> 3.67 us
    convert_element_type x14 -> x0, local copies, waits for them, and re-layouts: 3.02 us -> none  [the longest x12 2.74 us: store(): return lax.optimization_barrier(conv_out.astype(jnp.bfloat16))]
    pallas_call x0 -> x1, local copies, waits for them, and re-layouts: none -> 2.89 us  [body(): pl.pallas_call(functools.partial(kernel, sections, replicas), out_shape=j...]
  transfers between devices with their start and end apart: 1 -> 0, of which waited for: 1 -> 0; matrix products, arithmetic and copies ran while one was open for 0% -> 0% of each run, Pallas kernels for 0% -> 0%
where the time goes in v1:
time: 48.8 us; the launch traced here: 48.5 us
  Pallas kernels  42 us (86%)
  local copies, waits for them, and re-layouts  6.56 us (13%)
    pallas_call x1, Pallas kernels, body(): pl.pallas_call(functools.partial(kernel, sections, replicas), out_shape=j...  42 us
    unnamed x2, local copies, waits for them, and re-layouts  3.67 us
    pallas_call x1, local copies, waits for them, and re-layouts, body(): pl.pallas_call(functools.partial(kernel, sections, replicas), out_shape=j...  2.89 us

profile of v1, /device:TPU:3, one launch (start us, length us, event | category | flops | bytes accessed | tf_op | source)
XLA Modules:
  0.0 48.5 jit_solution(14169013906606658694)
XLA Ops:
  0.0 1.8 %copy.7.pend = bf16[1,2,14,14,512]{4,3,2,1,0:T(8,128)(2,1)} copy(bf16[1,2,14,14,512]{4,1,3,2,0:T(2,128)(2,1)} %param.6) | data formatting | bytes 802816 | tf_op args[0]
  1.8 1.8 %copy.8.arriving = bf16[1,2,14,14,512]{4,3,2,1,0:T(8,128)(2,1)} copy(bf16[1,2,14,14,512]{4,1,3,2,0:T(2,128)(2,1)} %param.7) | data formatting | bytes 802816 | tf_op args[1]
  3.7 42.0 %relay.1 = bf16[1,2,2,14,14,512]{5,4,3,2,1,0:T(8,128)(2,1)} custom-call(bf16[1,2,14,14,512]{4,3,2,1,0:T(8,128)(2,1)} %copy.7.pend, bf16[1,2,14,14,512]{4,3,2,1,0:T(8,128)(2,1)} %copy.8.arriving, bf16[1,3,3,512,512]{4,3,2,1,0:T(8,128)(2,1)} %first.1, bf16[1,3,3,512,512]{4,3,2,1,0:T(8,128)(2,1)} %second.1, f32[1,2,512]{2,1,0:T(2,128)} %gain.1, f32[1,2,512]{2,1,0:T(2,128)} %bias.1), custom_call_target="tpu_custom_call" | custom-call | flops 7398752256 | bytes 9437184 | tf_op jit(solution)/shard_map/relay/pallas_call | solution.py:327
  45.6 2.9 %copy.9 = bf16[1,2,2,14,14,512]{5,2,4,3,1,0:T(2,128)(2,1)} copy(bf16[1,2,2,14,14,512]{5,4,3,2,1,0:T(8,128)(2,1)} %relay.1) | data formatting | bytes 1605632 | tf_op jit(solution)/shard_map/relay/pallas_call | solution.py:327

commit v2 on v1

v2 whole, which is shorter than its diff:
```python
import functools

import jax
import jax.numpy as jnp
from jax import lax
from jax.experimental import pallas as pl
from jax.experimental.pallas import tpu as pltpu
from jax.sharding import PartitionSpec as P

MESH = pl.DeviceIdType.MESH
F32 = jnp.float32
BF16 = jnp.bfloat16
LANES = 128
SLOTS = 16
TILE = 256


def kernel(
    sections,
    replicas,
    pend,
    arriving,
    first,
    second,
    gain,
    bias,
    out,
    maps,
    weights,
    taps,
    y,
    sent,
    landed,
    mine,
    slots,
    coef,
    moved_coef,
    affine,
    result,
    map_sem,
    weight_sem,
    out_sem,
    stat_send,
    stat_recv,
    bulk_send,
    bulk_recv,
    coef_send,
    coef_recv,
):
    rows, _, images, _ = maps.shape[2:]
    cols, channels = pend.shape[2], pend.shape[4]
    pitch = SLOTS * images
    chunks = channels // LANES
    halves = channels // TILE
    cells = images * rows * cols
    sec = lax.axis_index("section")
    me = lax.axis_index("replica")

    barrier = pltpu.get_barrier_semaphore()

    def greet(d, carry):
        peer = lax.rem(me + d, replicas)
        pl.semaphore_signal(
            barrier, inc=1, device_id={"section": sec, "replica": peer}, device_id_type=MESH
        )
        return carry

    lax.fori_loop(1, replicas, greet, 0)

    @pl.when(sec > 0)
    def _():
        pl.semaphore_signal(
            barrier, inc=1, device_id={"section": sec - 1, "replica": me}, device_id_type=MESH
        )

    @pl.when(sec < sections - 1)
    def _():
        pl.semaphore_signal(
            barrier, inc=1, device_id={"section": sec + 1, "replica": me}, device_id_type=MESH
        )

    def lanes(k):
        return slice(k * LANES, (k + 1) * LANES)

    map_copies = [
        [
            pltpu.make_async_copy(
                src.at[0, :, :, :, pl.ds(k * LANES, LANES)],
                maps.at[which, k, :, pl.ds(0, cols)],
                map_sem.at[which, k],
            )
            for k in range(chunks)
        ]
        for which, src in enumerate((pend, arriving))
    ]
    out_copies = [
        [
            pltpu.make_async_copy(
                result.at[tick, k, :, pl.ds(0, cols)],
                out.at[0, tick, :, :, :, pl.ds(k * LANES, LANES)],
                out_sem.at[tick, k],
            )
            for k in range(chunks)
        ]
        for tick in range(2)
    ]
    flat_maps = maps.reshape(2, chunks, rows * pitch, LANES)
    flat_result = result.reshape(2, chunks, rows * pitch, LANES)
    weight_copies = [
        [
            pltpu.make_async_copy(src.at[0, dy], weights.at[layer, dy], weight_sem.at[layer, dy])
            for dy in range(3)
        ]
        for layer, src in enumerate((first, second))
    ]
    for copy in map_copies[0]:
        copy.start()
    for layer in range(2):
        for dy in range(3):
            weight_copies[layer][dy].start()
    for copy in map_copies[1]:
        copy.start()

    for layer in range(2):
        for k in range(chunks):
            lane = slice(k * LANES, (k + 1) * LANES)
            affine[layer, k : k + 1, :] = gain[0, layer : layer + 1, lane]
            affine[layer, chunks + k : chunks + k + 1, :] = bias[0, layer : layer + 1, lane]

    pad = jnp.zeros((halves, pitch, 3 * TILE), BF16)
    taps[:, 0:pitch, :] = pad
    taps[:, (rows + 1) * pitch : (rows + 2) * pitch, :] = pad

    inside = (
        lax.broadcasted_iota(jnp.int32, (rows, pitch, LANES), 1).reshape(rows * pitch, LANES)
        < cols * images
    )

    def lay(k, values):
        flat = jnp.where(inside, values, 0.0)
        half, lane = (k * LANES) // TILE, (k * LANES) % TILE
        where = slice(pitch, (rows + 1) * pitch)
        taps[half, where, lane : lane + LANES] = pltpu.roll(flat, images, 0).astype(BF16)
        taps[half, where, TILE + lane : TILE + lane + LANES] = flat.astype(BF16)
        taps[half, where, 2 * TILE + lane : 2 * TILE + lane + LANES] = pltpu.roll(
            flat, rows * pitch - images, 0
        ).astype(BF16)

    def lay_maps(which):
        for k in range(chunks):
            lay(k, flat_maps[which, k].astype(F32))

    def multiply(layer, parts, add):
        total = None
        for dy, half in parts:
            left = taps[half, dy * pitch : (dy + rows) * pitch, :]
            right = weights[layer, dy, :, half * TILE : (half + 1) * TILE, :]
            term = jnp.dot(
                left, right.reshape(3 * TILE, channels), preferred_element_type=F32
            )
            total = term if total is None else total + term
        y[...] = y[...] + total if add else total

    every = [(dy, half) for half in range(halves) for dy in range(3)]

    def gather_statistics(phase):
        for k in range(chunks):
            total = jnp.sum(jnp.where(inside, y[:, lanes(k)], 0.0), axis=0, keepdims=True)
            mean = total / cells
            centred = jnp.where(inside, y[:, lanes(k)] - mean, 0.0)
            mine[phase, k : k + 1, :] = mean
            mine[phase, chunks + k : chunks + k + 1, :] = jnp.sum(
                centred * centred, axis=0, keepdims=True
            )

    def send_statistics(phase):
        def send(d, carry):
            peer = lax.rem(me + d, replicas)
            pltpu.make_async_remote_copy(
                src_ref=mine.at[phase],
                dst_ref=slots.at[phase, d - 1],
                send_sem=stat_send.at[phase],
                recv_sem=stat_recv.at[phase],
                device_id={"section": sec, "replica": peer},
                device_id_type=MESH,
            ).start()
            return carry

        lax.fori_loop(1, replicas, send, 0)

    def combine(phase, layer):
        pltpu.make_async_copy(slots.at[phase], slots.at[phase], stat_recv.at[phase]).wait()
        own = mine[phase]
        others = slots[phase]
        total = own + jnp.sum(others, axis=0)
        mean = total[0:chunks] / replicas
        apart = (own[0:chunks] - mean) ** 2 + jnp.sum(
            (others[:, 0:chunks] - mean[None]) ** 2, axis=0
        )
        var = (total[chunks:] + apart * cells) / (cells * replicas)
        scale = affine[layer, 0:chunks, :] * lax.rsqrt(var + 1e-05)
        coef[phase, 0:chunks, :] = scale
        coef[phase, chunks:, :] = affine[layer, chunks:, :] - mean * scale

    def activate(values, table, k):
        scale = table[k : k + 1, :]
        offset = table[chunks + k : chunks + k + 1, :]
        return jnp.maximum(values * scale + offset, 0.0)

    def lay_hidden(phase):
        table = coef[phase]
        for k in range(chunks):
            lay(k, activate(y[:, lanes(k)], table, k))

    def give_result(tick, phase):
        table = coef[phase]
        for k in range(chunks):
            flat_result[tick, k] = activate(y[:, lanes(k)], table, k).astype(BF16)
            out_copies[tick][k].start()

    for copy in map_copies[0]:
        copy.wait()
    lay_maps(0)
    for dy in range(3):
        weight_copies[0][dy].wait()
        multiply(0, [(dy, half) for half in range(halves)], dy > 0)
    gather_statistics(0)
    pl.semaphore_wait(
        barrier,
        replicas - 1 + (sec > 0).astype(jnp.int32) + (sec < sections - 1).astype(jnp.int32),
    )
    send_statistics(0)
    for dy in range(3):
        weight_copies[1][dy].wait()
    for copy in map_copies[1]:
        copy.wait()
    combine(0, 0)
    lay_hidden(0)

    def bulk(n):
        return pltpu.make_async_remote_copy(
            src_ref=sent.at[n],
            dst_ref=landed.at[n],
            send_sem=bulk_send.at[n],
            recv_sem=bulk_recv.at[n],
            device_id={"section": sec + 1, "replica": me},
            device_id_type=MESH,
        )

    def coefficients():
        return pltpu.make_async_remote_copy(
            src_ref=coef.at[1],
            dst_ref=moved_coef,
            send_sem=coef_send,
            recv_sem=coef_recv,
            device_id={"section": sec + 1, "replica": me},
            device_id_type=MESH,
        )

    multiply(1, every, False)
    for n in range(halves):
        sent[n] = y[:, n * TILE : (n + 1) * TILE].astype(BF16)

        @pl.when(sec < sections - 1)
        def _():
            bulk(n).start()

    gather_statistics(1)
    send_statistics(1)
    combine(1, 1)

    @pl.when(sec < sections - 1)
    def _():
        coefficients().start()

    give_result(0, 1)

    @pl.when(sec == 0)
    def _():
        lay_maps(1)

    def lay_landed(half):
        bulk(half).wait_recv()
        table = moved_coef[...]
        for k in range(half * TILE // LANES, (half + 1) * TILE // LANES):
            at = k * LANES - half * TILE
            values = landed[half, :, at : at + LANES].astype(F32)
            lay(k, activate(values, table, k))

    for half in range(halves):

        @pl.when(sec > 0)
        def _():
            if half == 0:
                coefficients().wait_recv()
            lay_landed(half)

        multiply(0, [(dy, half) for dy in range(3)], half > 0)
    gather_statistics(2)
    send_statistics(2)
    combine(2, 0)
    lay_hidden(2)

    multiply(1, every, False)
    gather_statistics(3)
    send_statistics(3)
    combine(3, 1)
    give_result(1, 3)

    for phase in range(4):
        pltpu.make_async_copy(slots.at[phase], slots.at[phase], stat_send.at[phase]).wait()

    @pl.when(sec < sections - 1)
    def _():
        for n in range(halves):
            bulk(n).wait_send()
        coefficients().wait_send()

    for copies in out_copies:
        for copy in copies:
            copy.wait()


def solution(mesh):
    sections, replicas = mesh.shape["section"], mesh.shape["replica"]

    def body(pend, arriving, first, second, gain, bias):
        images, rows, cols, channels = pend.shape[1:]
        pend = jnp.transpose(pend, (0, 2, 3, 1, 4))
        arriving = jnp.transpose(arriving, (0, 2, 3, 1, 4))
        pitch = SLOTS * images
        chunks = channels // LANES
        halves = channels // TILE
        tile = 2 * channels // LANES
        dma = pltpu.SemaphoreType.DMA
        anywhere = pl.BlockSpec(memory_space=pl.ANY)
        vmem = pl.BlockSpec(memory_space=pltpu.VMEM)
        depth = 9 * channels * channels
        produced = pl.pallas_call(
            functools.partial(kernel, sections, replicas),
            out_shape=jax.ShapeDtypeStruct((1, 2, rows, cols, images, channels), BF16),
            in_specs=[anywhere] * 4 + [vmem] * 2,
            out_specs=anywhere,
            scratch_shapes=[
                pltpu.VMEM((2, chunks, rows, SLOTS, images, LANES), BF16),
                pltpu.VMEM((2, 3, 3, channels, channels), BF16),
                pltpu.VMEM((halves, (rows + 2) * pitch, 3 * TILE), BF16),
                pltpu.VMEM((rows * pitch, channels), F32),
                pltpu.VMEM((halves, rows * pitch, TILE), BF16),
                pltpu.VMEM((halves, rows * pitch, TILE), BF16),
                pltpu.VMEM((4, tile, LANES), F32),
                pltpu.VMEM((4, replicas - 1, tile, LANES), F32),
                pltpu.VMEM((4, tile, LANES), F32),
                pltpu.VMEM((tile, LANES), F32),
                pltpu.VMEM((2, tile, LANES), F32),
                pltpu.VMEM((2, chunks, rows, SLOTS, images, LANES), BF16),
                dma((2, chunks)),
                dma((2, 3)),
                dma((2, chunks)),
                dma((4,)),
                dma((4,)),
                dma((halves,)),
                dma((halves,)),
                dma,
                dma,
            ],
            compiler_params=pltpu.CompilerParams(
                collective_id=0, has_side_effects=True, vmem_limit_bytes=56 * 2**20
            ),
            cost_estimate=pl.CostEstimate(
                flops=8 * images * rows * cols * depth,
                bytes_accessed=4 * depth,
                transcendentals=0,
            ),
            name="relay",
        )(pend, arriving, first, second, gain, bias)
        return jnp.transpose(produced, (0, 1, 4, 2, 3, 5))

    in_specs = (
        P("section", "replica", None, None, None),
        P(None, "replica", None, None, None),
        P("section", None, None, None, None),
        P("section", None, None, None, None),
        P("section", None, None),
        P("section", None, None),
    )
    out_specs = P("section", None, "replica", None, None, None)
    return jax.shard_map(body, mesh=mesh, in_specs=in_specs, out_specs=out_specs, check_vma=False)
```

time: 48.8 us -> 43.1 us (0.88)
  local copies, waits for them, and re-layouts: 6.56 us -> 2.58 us
  Pallas kernels: 42 us -> 40.3 us
    pallas_call x1 -> x0, local copies, waits for them, and re-layouts: 2.89 us -> none  [body(): pl.pallas_call(functools.partial(kernel, sections, replicas), out_shape=j...]
    pallas_call x1, Pallas kernels: 42 us -> 40.3 us  [body(): pl.pallas_call(functools.partial(kernel, sections, replicas), out_shape=j...]
    unnamed x2 -> x1, local copies, waits for them, and re-layouts: 3.67 us -> 2.58 us
where the time goes in v2:
time: 43.1 us; the launch traced here: 42.9 us
  Pallas kernels  40.3 us (94%)
  local copies, waits for them, and re-layouts  2.58 us (6%)
    pallas_call x1, Pallas kernels, body(): pl.pallas_call(functools.partial(kernel, sections, replicas), out_shape=j...  40.3 us
    unnamed x1, local copies, waits for them, and re-layouts  2.58 us

profile of v2, /device:TPU:3, one launch (start us, length us, event | category | flops | bytes accessed | tf_op | source)
XLA Modules:
  0.0 42.9 jit_solution(1684139164659369547)
XLA Ops:
  0.0 40.3 %relay.1 = bf16[1,2,14,14,2,512]{5,4,3,2,1,0:T(2,128)(2,1)} custom-call(bf16[1,14,14,2,512]{4,3,2,1,0:T(2,128)(2,1)} %bitcast.4, bf16[1,14,14,2,512]{4,3,2,1,0:T(2,128)(2,1)} %bitcast.5, bf16[1,3,3,512,512]{4,3,2,1,0:T(8,128)(2,1)} %first.1, bf16[1,3,3,512,512]{4,3,2,1,0:T(8,128)(2,1)} %second.1, f32[1,2,512]{2,1,0:T(2,128)} %gain.1, f32[1,2,512]{2,1,0:T(2,128)} %bias.1), custom_call_target="tpu_custom_call" | custom-call | flops 7398752256 | bytes 9437184 | tf_op jit(solution)/shard_map/relay/pallas_call | solution.py:339
  40.3 2.6 %copy.8 = bf16[1,2,2,14,14,512]{5,2,4,3,1,0:T(2,128)(2,1)} copy(bf16[1,2,2,14,14,512]{5,2,4,3,1,0:T(2,128)(2,1)} %bitcast.3) | data formatting | bytes 1605632

commit v3 on v2

v3 whole, which is shorter than its diff:
```python
import functools

import jax
import jax.numpy as jnp
from jax import lax
from jax.experimental import pallas as pl
from jax.experimental.pallas import tpu as pltpu
from jax.sharding import PartitionSpec as P

MESH = pl.DeviceIdType.MESH
F32 = jnp.float32
BF16 = jnp.bfloat16
LANES = 128
SLOTS = 16
TILE = 256


def kernel(
    sections,
    replicas,
    pend,
    arriving,
    first,
    second,
    gain,
    bias,
    out,
    maps,
    weights,
    taps,
    y,
    sent,
    landed,
    mine,
    slots,
    coef,
    moved_coef,
    affine,
    result,
    map_sem,
    weight_sem,
    out_sem,
    stat_send,
    stat_recv,
    bulk_send,
    bulk_recv,
    coef_send,
    coef_recv,
):
    rows, _, images, _ = maps.shape[2:]
    cols, channels = pend.shape[2], pend.shape[4]
    pitch = SLOTS * images
    chunks = channels // LANES
    halves = channels // TILE
    per = TILE // LANES
    cells = images * rows * cols
    sec = lax.axis_index("section")
    me = lax.axis_index("replica")

    barrier = pltpu.get_barrier_semaphore()

    def greet(d, carry):
        peer = lax.rem(me + d, replicas)
        pl.semaphore_signal(
            barrier, inc=1, device_id={"section": sec, "replica": peer}, device_id_type=MESH
        )
        return carry

    lax.fori_loop(1, replicas, greet, 0)

    @pl.when(sec > 0)
    def _():
        pl.semaphore_signal(
            barrier, inc=1, device_id={"section": sec - 1, "replica": me}, device_id_type=MESH
        )

    @pl.when(sec < sections - 1)
    def _():
        pl.semaphore_signal(
            barrier, inc=1, device_id={"section": sec + 1, "replica": me}, device_id_type=MESH
        )

    def lanes(k):
        return slice(k * LANES, (k + 1) * LANES)

    map_copies = [
        [
            pltpu.make_async_copy(
                src.at[0, :, :, :, pl.ds(k * LANES, LANES)],
                maps.at[which, k, :, pl.ds(0, cols)],
                map_sem.at[which, k],
            )
            for k in range(chunks)
        ]
        for which, src in enumerate((pend, arriving))
    ]
    out_copies = [
        [
            pltpu.make_async_copy(
                result.at[tick, k, :, pl.ds(0, cols)],
                out.at[0, tick, :, :, :, pl.ds(k * LANES, LANES)],
                out_sem.at[tick, k],
            )
            for k in range(chunks)
        ]
        for tick in range(2)
    ]
    flat_maps = maps.reshape(2, chunks, rows * pitch, LANES)
    flat_result = result.reshape(2, chunks, rows * pitch, LANES)
    flat_sent = sent.reshape(chunks, rows * pitch, LANES)
    flat_landed = landed.reshape(chunks, rows * pitch, LANES)
    weight_copies = [
        [
            pltpu.make_async_copy(src.at[0, dy], weights.at[layer, dy], weight_sem.at[layer, dy])
            for dy in range(3)
        ]
        for layer, src in enumerate((first, second))
    ]
    for copy in map_copies[0]:
        copy.start()
    for layer in range(2):
        for dy in range(3):
            weight_copies[layer][dy].start()
    for copy in map_copies[1]:
        copy.start()

    for layer in range(2):
        for k in range(chunks):
            lane = slice(k * LANES, (k + 1) * LANES)
            g, j = divmod(k, per)
            affine[layer, g, j : j + 1, :] = gain[0, layer : layer + 1, lane]
            affine[layer, g, per + j : per + j + 1, :] = bias[0, layer : layer + 1, lane]

    pad = jnp.zeros((halves, pitch, 3 * TILE), BF16)
    taps[:, 0:pitch, :] = pad
    taps[:, (rows + 1) * pitch : (rows + 2) * pitch, :] = pad

    inside = (
        lax.broadcasted_iota(jnp.int32, (rows, pitch, LANES), 1).reshape(rows * pitch, LANES)
        < cols * images
    )

    def lay(k, values):
        flat = jnp.where(inside, values, 0.0)
        half, lane = (k * LANES) // TILE, (k * LANES) % TILE
        where = slice(pitch, (rows + 1) * pitch)
        taps[half, where, lane : lane + LANES] = pltpu.roll(flat, images, 0).astype(BF16)
        taps[half, where, TILE + lane : TILE + lane + LANES] = flat.astype(BF16)
        taps[half, where, 2 * TILE + lane : 2 * TILE + lane + LANES] = pltpu.roll(
            flat, rows * pitch - images, 0
        ).astype(BF16)

    def lay_maps(which):
        for k in range(chunks):
            lay(k, flat_maps[which, k].astype(F32))

    def multiply(which, layer, parts, group, add):
        lane = slice(0, channels) if group is None else slice(group * TILE, (group + 1) * TILE)
        total = None
        for dy, half in parts:
            left = taps[half, dy * pitch : (dy + rows) * pitch, :]
            right = weights[layer, dy, :, half * TILE : (half + 1) * TILE, lane]
            term = jnp.dot(
                left,
                right.reshape(3 * TILE, lane.stop - lane.start),
                preferred_element_type=F32,
            )
            total = term if total is None else total + term
        y[which, :, lane] = y[which, :, lane] + total if add else total

    def taps_of(half):
        return [(dy, half) for dy in range(3)]

    def send_statistics(which, phase, g):
        for j in range(per):
            lane = lanes(g * per + j)
            total = jnp.sum(jnp.where(inside, y[which, :, lane], 0.0), axis=0, keepdims=True)
            mean = total / cells
            centred = jnp.where(inside, y[which, :, lane] - mean, 0.0)
            mine[phase, g, j : j + 1, :] = mean
            mine[phase, g, per + j : per + j + 1, :] = jnp.sum(
                centred * centred, axis=0, keepdims=True
            )

        def send(d, carry):
            peer = lax.rem(me + d, replicas)
            pltpu.make_async_remote_copy(
                src_ref=mine.at[phase, g],
                dst_ref=slots.at[phase, g, d - 1],
                send_sem=stat_send.at[phase, g],
                recv_sem=stat_recv.at[phase, g],
                device_id={"section": sec, "replica": peer},
                device_id_type=MESH,
            ).start()
            return carry

        lax.fori_loop(1, replicas, send, 0, unroll=replicas <= 16)

    def combine(phase, layer, g):
        here = slots.at[phase, g]
        pltpu.make_async_copy(here, here, stat_recv.at[phase, g]).wait()
        own = mine[phase, g]
        others = slots[phase, g]
        total = own + jnp.sum(others, axis=0)
        mean = total[0:per] / replicas
        apart = (own[0:per] - mean) ** 2 + jnp.sum((others[:, 0:per] - mean[None]) ** 2, axis=0)
        var = (total[per:] + apart * cells) / (cells * replicas)
        scale = affine[layer, g, 0:per, :] * lax.rsqrt(var + 1e-05)
        coef[phase, g, 0:per, :] = scale
        coef[phase, g, per:, :] = affine[layer, g, per:, :] - mean * scale

    def activate(values, table, j):
        return jnp.maximum(values * table[j : j + 1, :] + table[per + j : per + j + 1, :], 0.0)

    def lay_hidden(which, phase, g):
        table = coef[phase, g]
        for j in range(per):
            k = g * per + j
            lay(k, activate(y[which, :, lanes(k)], table, j))

    def give_result(which, tick, phase, g):
        table = coef[phase, g]
        for j in range(per):
            k = g * per + j
            flat_result[tick, k] = activate(y[which, :, lanes(k)], table, j).astype(BF16)
            out_copies[tick][k].start()

    def bulk(k):
        return pltpu.make_async_remote_copy(
            src_ref=sent.at[k, :, pl.ds(0, cols)],
            dst_ref=landed.at[k, :, pl.ds(0, cols)],
            send_sem=bulk_send.at[k],
            recv_sem=bulk_recv.at[k],
            device_id={"section": sec + 1, "replica": me},
            device_id_type=MESH,
        )

    def coefficients(g):
        return pltpu.make_async_remote_copy(
            src_ref=coef.at[1, g],
            dst_ref=moved_coef.at[g],
            send_sem=coef_send.at[g],
            recv_sem=coef_recv.at[g],
            device_id={"section": sec + 1, "replica": me},
            device_id_type=MESH,
        )

    has_next = sec < sections - 1
    has_previous = sec > 0

    for copy in map_copies[0]:
        copy.wait()
    lay_maps(0)
    for dy in range(3):
        weight_copies[0][dy].wait()
        parts = [(dy, half) for half in range(halves)]
        if dy < 2:
            multiply(0, 0, parts, None, dy > 0)
    for g in range(halves):
        multiply(0, 0, parts, g, True)
        if g == 0:
            pl.semaphore_wait(
                barrier,
                replicas - 1 + has_previous.astype(jnp.int32) + has_next.astype(jnp.int32),
            )
        send_statistics(0, 0, g)
    for dy in range(3):
        weight_copies[1][dy].wait()
    for copy in map_copies[1]:
        copy.wait()

    for half in range(halves):
        combine(0, 0, half)
        lay_hidden(0, 0, half)
        multiply(1, 1, taps_of(half), 0, half > 0)
    for g in range(halves):
        if g > 0:
            for half in range(halves):
                multiply(1, 1, taps_of(half), g, half > 0)
        for j in range(per):
            k = g * per + j
            flat_sent[k] = y[1, :, lanes(k)].astype(BF16)

        @pl.when(has_next)
        def _():
            for k in range(g * per, (g + 1) * per):
                if k < chunks - 1:
                    bulk(k).start()

        send_statistics(1, 1, g)
    for g in range(halves):
        combine(1, 1, g)

        @pl.when(has_next)
        def _():
            coefficients(g).start()
            if g == 0:
                bulk(chunks - 1).start()

    for g in range(halves):
        give_result(1, 0, 1, g)

    @pl.when(sec == 0)
    def _():
        lay_maps(1)

    for half in range(halves):

        @pl.when(has_previous)
        def _():
            coefficients(half).wait_recv()
            table = moved_coef[half]
            for j in range(per):
                k = half * per + j
                bulk(k).wait_recv()
                lay(k, activate(flat_landed[k].astype(F32), table, j))

        if half < halves - 1:
            multiply(0, 0, taps_of(half), None, half > 0)
    for g in range(halves):
        multiply(0, 0, taps_of(halves - 1), g, halves > 1)
        send_statistics(0, 2, g)

    for half in range(halves):
        combine(2, 0, half)
        lay_hidden(0, 2, half)
        if half < halves - 1:
            multiply(1, 1, taps_of(half), None, half > 0)
    for g in range(halves):
        multiply(1, 1, taps_of(halves - 1), g, halves > 1)
        send_statistics(1, 3, g)
    for g in range(halves):
        combine(3, 1, g)
        give_result(1, 1, 3, g)

    for phase in range(4):
        for g in range(halves):
            here = slots.at[phase, g]
            pltpu.make_async_copy(here, here, stat_send.at[phase, g]).wait()

    @pl.when(has_next)
    def _():
        for k in range(chunks):
            bulk(k).wait_send()
        for g in range(halves):
            coefficients(g).wait_send()

    for copies in out_copies:
        for copy in copies:
            copy.wait()


def hand_over(given, out, sems):
    ticks, rows = given.shape[1:3]
    cut = (rows + 1) // 2
    copies = []
    for tick in range(ticks):
        for n, part in enumerate((pl.ds(0, cut), pl.ds(cut, rows - cut))):
            copies.append(
                pltpu.make_async_copy(
                    given.at[0, tick, part], out.at[0, tick, part], sems.at[tick, n]
                )
            )
    for copy in copies:
        copy.start()
    for copy in copies:
        copy.wait()


def solution(mesh):
    sections, replicas = mesh.shape["section"], mesh.shape["replica"]

    def body(pend, arriving, first, second, gain, bias):
        images, rows, cols, channels = pend.shape[1:]
        pend = jnp.transpose(pend, (0, 2, 3, 1, 4))
        arriving = jnp.transpose(arriving, (0, 2, 3, 1, 4))
        pitch = SLOTS * images
        chunks = channels // LANES
        halves = channels // TILE
        tile = 2 * TILE // LANES
        limit = 56 * 2**20
        dma = pltpu.SemaphoreType.DMA
        anywhere = pl.BlockSpec(memory_space=pl.ANY)
        vmem = pl.BlockSpec(memory_space=pltpu.VMEM)
        depth = 9 * channels * channels
        produced = pl.pallas_call(
            functools.partial(kernel, sections, replicas),
            out_shape=jax.ShapeDtypeStruct((1, 2, rows, cols, images, channels), BF16),
            in_specs=[anywhere] * 4 + [vmem] * 2,
            out_specs=anywhere,
            scratch_shapes=[
                pltpu.VMEM((2, chunks, rows, SLOTS, images, LANES), BF16),
                pltpu.VMEM((2, 3, 3, channels, channels), BF16),
                pltpu.VMEM((halves, (rows + 2) * pitch, 3 * TILE), BF16),
                pltpu.VMEM((2, rows * pitch, channels), F32),
                pltpu.VMEM((chunks, rows, SLOTS, images, LANES), BF16),
                pltpu.VMEM((chunks, rows, SLOTS, images, LANES), BF16),
                pltpu.VMEM((4, halves, tile, LANES), F32),
                pltpu.VMEM((4, halves, replicas - 1, tile, LANES), F32),
                pltpu.VMEM((4, halves, tile, LANES), F32),
                pltpu.VMEM((halves, tile, LANES), F32),
                pltpu.VMEM((2, halves, tile, LANES), F32),
                pltpu.VMEM((2, chunks, rows, SLOTS, images, LANES), BF16),
                dma((2, chunks)),
                dma((2, 3)),
                dma((2, chunks)),
                dma((4, halves)),
                dma((4, halves)),
                dma((chunks,)),
                dma((chunks,)),
                dma((halves,)),
                dma((halves,)),
            ],
            compiler_params=pltpu.CompilerParams(
                collective_id=0, has_side_effects=True, vmem_limit_bytes=limit
            ),
            cost_estimate=pl.CostEstimate(
                flops=8 * images * rows * cols * depth,
                bytes_accessed=4 * depth,
                transcendentals=0,
            ),
            name="relay",
        )(pend, arriving, first, second, gain, bias)
        produced = pl.pallas_call(
            hand_over,
            out_shape=jax.ShapeDtypeStruct(produced.shape, BF16),
            in_specs=[anywhere],
            out_specs=anywhere,
            scratch_shapes=[dma((2, 2))],
            compiler_params=pltpu.CompilerParams(vmem_limit_bytes=limit),
            name="hand_over",
        )(produced)
        return jnp.transpose(produced, (0, 1, 4, 2, 3, 5))

    in_specs = (
        P("section", "replica", None, None, None),
        P(None, "replica", None, None, None),
        P("section", None, None, None, None),
        P("section", None, None, None, None),
        P("section", None, None),
        P("section", None, None),
    )
    out_specs = P("section", None, "replica", None, None, None)
    return jax.shard_map(body, mesh=mesh, in_specs=in_specs, out_specs=out_specs, check_vma=False)
```

time: 43.1 us -> 65.4 us (1.52)
  Pallas kernels: 40.3 us -> 65 us
  local copies, waits for them, and re-layouts: 2.58 us -> 0 us
    pallas_call x0 -> x1, Pallas kernels: none -> 25.5 us  [body(): pl.pallas_call(hand_over, out_shape=jax.ShapeDtypeStruct(produced.shape,...]
    unnamed x1 -> x0, local copies, waits for them, and re-layouts: 2.58 us -> none
    pallas_call x1, Pallas kernels: 40.3 us -> 39.6 us  [body(): pl.pallas_call(functools.partial(kernel, sections, replicas), out_shape=j...]
where the time goes in v3:
time: 65.4 us; the launch traced here: 65.2 us
  Pallas kernels  65 us (99%)
    pallas_call x1, Pallas kernels, body(): pl.pallas_call(functools.partial(kernel, sections, replicas), out_shape=j...  39.6 us
    pallas_call x1, Pallas kernels, body(): pl.pallas_call(hand_over, out_shape=jax.ShapeDtypeStruct(produced.shape,...  25.5 us

profile of v3, /device:TPU:3, one launch (start us, length us, event | category | flops | bytes accessed | tf_op | source)
XLA Modules:
  0.0 65.2 jit_solution(4439146195345797793)
XLA Ops:
  0.0 39.6 %relay.1.given = bf16[1,2,14,14,2,512]{5,4,3,2,1,0:T(2,128)(2,1)} custom-call(bf16[1,14,14,2,512]{4,3,2,1,0:T(2,128)(2,1)} %bitcast.3, bf16[1,14,14,2,512]{4,3,2,1,0:T(2,128)(2,1)} %bitcast.4, bf16[1,3,3,512,512]{4,3,2,1,0:T(8,128)(2,1)} %first.1, bf16[1,3,3,512,512]{4,3,2,1,0:T(8,128)(2,1)} %second.1, f32[1,2,512]{2,1,0:T(2,128)} %gain.1, f32[1,2,512]{2,1,0:T(2,128)} %bias.1), custom_call_target="tpu_custom_call" | custom-call | flops 7398752256 | bytes 9437184 | tf_op jit(solution)/shard_map/relay/pallas_call | solution.py:386
  39.6 25.5 %hand_over.1 = bf16[1,2,14,14,2,512]{5,4,3,2,1,0:T(2,128)(2,1)} custom-call(bf16[1,2,14,14,2,512]{5,4,3,2,1,0:T(2,128)(2,1)} %relay.1.given), custom_call_target="tpu_custom_call" | custom-call | tf_op jit(solution)/shard_map/hand_over/pallas_call | solution.py:424

commit v4 on v2

--- a/solution.py
+++ b/solution.py
@@ -52,6 +52,7 @@
     pitch = SLOTS * images
     chunks = channels // LANES
     halves = channels // TILE
+    per = TILE // LANES
     cells = images * rows * cols
     sec = lax.axis_index("section")
     me = lax.axis_index("replica")
@@ -80,7 +81,10 @@
         )
 
     def lanes(k):
-        return slice(k * LANES, (k + 1) * LANES)
+        return pl.ds(pl.multiple_of(k * LANES, LANES), LANES)
+
+    def each(count, step):
+        lax.fori_loop(0, count, lambda i, carry: step(i), None)
 
     map_copies = [
         [
@@ -106,6 +110,8 @@
     ]
     flat_maps = maps.reshape(2, chunks, rows * pitch, LANES)
     flat_result = result.reshape(2, chunks, rows * pitch, LANES)
+    flat_sent = sent.reshape(chunks, rows * pitch, LANES)
+    flat_landed = landed.reshape(chunks, rows * pitch, LANES)
     weight_copies = [
         [
             pltpu.make_async_copy(src.at[0, dy], weights.at[layer, dy], weight_sem.at[layer, dy])
@@ -138,42 +144,54 @@
 
     def lay(k, values):
         flat = jnp.where(inside, values, 0.0)
-        half, lane = (k * LANES) // TILE, (k * LANES) % TILE
-        where = slice(pitch, (rows + 1) * pitch)
-        taps[half, where, lane : lane + LANES] = pltpu.roll(flat, images, 0).astype(BF16)
-        taps[half, where, TILE + lane : TILE + lane + LANES] = flat.astype(BF16)
-        taps[half, where, 2 * TILE + lane : 2 * TILE + lane + LANES] = pltpu.roll(
-            flat, rows * pitch - images, 0
-        ).astype(BF16)
+        half, lane = k // per, (k % per) * LANES
+        shifted = (pltpu.roll(flat, images, 0), flat, pltpu.roll(flat, rows * pitch - images, 0))
+        for dx, tap in enumerate(shifted):
+            at = pl.multiple_of(dx * TILE + lane, LANES)
+            taps[half, pitch : (rows + 1) * pitch, pl.ds(at, LANES)] = tap.astype(BF16)
 
     def lay_maps(which):
-        for k in range(chunks):
-            lay(k, flat_maps[which, k].astype(F32))
-
-    def multiply(layer, parts, add):
-        total = None
-        for dy, half in parts:
-            left = taps[half, dy * pitch : (dy + rows) * pitch, :]
-            right = weights[layer, dy, :, half * TILE : (half + 1) * TILE, :]
-            term = jnp.dot(
-                left, right.reshape(3 * TILE, channels), preferred_element_type=F32
-            )
-            total = term if total is None else total + term
-        y[...] = y[...] + total if add else total
-
-    every = [(dy, half) for half in range(halves) for dy in range(3)]
-
-    def gather_statistics(phase):
-        for k in range(chunks):
+        each(chunks, lambda k: lay(k, flat_maps[which, k].astype(F32)))
+
+    def product(layer, dy, half, lane, width):
+        left = taps[half, pl.ds(pl.multiple_of(dy * pitch, pitch), rows * pitch), :]
+        right = weights[layer, dy, :, half * TILE : (half + 1) * TILE, lane : lane + width]
+        return jnp.dot(left, right.reshape(3 * TILE, width), preferred_element_type=F32)
+
+    def multiply(layer, parts, lane=0, width=channels, add=False, ready=None):
+        where = slice(lane, lane + width)
+        if not add:
+            y[:, where] = jnp.zeros((rows * pitch, width), F32)
+
+        def step(dy):
+            if ready is not None:
+                ready(dy)
+            total = y[:, where]
+            for half in parts:
+                total = total + product(layer, dy, half, lane, width)
+            y[:, where] = total
+
+        each(3, step)
+
+    everything = range(halves)
+
+    def send_statistics(phase):
+        def measure(k):
             total = jnp.sum(jnp.where(inside, y[:, lanes(k)], 0.0), axis=0, keepdims=True)
             mean = total / cells
             centred = jnp.where(inside, y[:, lanes(k)] - mean, 0.0)
-            mine[phase, k : k + 1, :] = mean
-            mine[phase, chunks + k : chunks + k + 1, :] = jnp.sum(
+            mine[phase, pl.ds(k, 1), :] = mean
+            mine[phase, pl.ds(chunks + k, 1), :] = jnp.sum(
                 centred * centred, axis=0, keepdims=True
             )
 
-    def send_statistics(phase):
+        each(chunks, measure)
+        if phase == 0:
+            pl.semaphore_wait(
+                barrier,
+                replicas - 1 + has_previous.astype(jnp.int32) + has_next.astype(jnp.int32),
+            )
+
         def send(d, carry):
             peer = lax.rem(me + d, replicas)
             pltpu.make_async_remote_copy(
@@ -189,7 +207,8 @@
         lax.fori_loop(1, replicas, send, 0)
 
     def combine(phase, layer):
-        pltpu.make_async_copy(slots.at[phase], slots.at[phase], stat_recv.at[phase]).wait()
+        here = slots.at[phase]
+        pltpu.make_async_copy(here, here, stat_recv.at[phase]).wait()
         own = mine[phase]
         others = slots[phase]
         total = own + jnp.sum(others, axis=0)
@@ -203,31 +222,53 @@
         coef[phase, chunks:, :] = affine[layer, chunks:, :] - mean * scale
 
     def activate(values, table, k):
-        scale = table[k : k + 1, :]
-        offset = table[chunks + k : chunks + k + 1, :]
+        scale = table[pl.ds(k, 1), :]
+        offset = table[pl.ds(chunks + k, 1), :]
         return jnp.maximum(values * scale + offset, 0.0)
 
     def lay_hidden(phase):
-        table = coef[phase]
-        for k in range(chunks):
-            lay(k, activate(y[:, lanes(k)], table, k))
+        each(chunks, lambda k: lay(k, activate(y[:, lanes(k)], coef.at[phase], k)))
 
     def give_result(tick, phase):
-        table = coef[phase]
-        for k in range(chunks):
-            flat_result[tick, k] = activate(y[:, lanes(k)], table, k).astype(BF16)
-            out_copies[tick][k].start()
+        def give(k):
+            flat_result[tick, k] = activate(y[:, lanes(k)], coef.at[phase], k).astype(BF16)
+
+        each(chunks, give)
+        for copy in out_copies[tick]:
+            copy.start()
+
+    def bulk(k):
+        return pltpu.make_async_remote_copy(
+            src_ref=sent.at[k, :, pl.ds(0, cols)],
+            dst_ref=landed.at[k, :, pl.ds(0, cols)],
+            send_sem=bulk_send.at[k],
+            recv_sem=bulk_recv.at[k],
+            device_id={"section": sec + 1, "replica": me},
+            device_id_type=MESH,
+        )
+
+    def coefficients():
+        return pltpu.make_async_remote_copy(
+            src_ref=coef.at[1],
+            dst_ref=moved_coef,
+            send_sem=coef_send,
+            recv_sem=coef_recv,
+            device_id={"section": sec + 1, "replica": me},
+            device_id_type=MESH,
+        )
+
+    has_next = sec < sections - 1
+    has_previous = sec > 0
 
     for copy in map_copies[0]:
         copy.wait()
     lay_maps(0)
-    for dy in range(3):
-        weight_copies[0][dy].wait()
-        multiply(0, [(dy, half) for half in range(halves)], dy > 0)
-    gather_statistics(0)
-    pl.semaphore_wait(
-        barrier,
-        replicas - 1 + (sec > 0).astype(jnp.int32) + (sec < sections - 1).astype(jnp.int32),
+    multiply(
+        0,
+        everything,
+        ready=lambda dy: pltpu.make_async_copy(
+            first.at[0, dy], weights.at[0, dy], weight_sem.at[0, dy]
+        ).wait(),
     )
     send_statistics(0)
     for dy in range(3):
@@ -237,41 +278,24 @@
     combine(0, 0)
     lay_hidden(0)
 
-    def bulk(n):
-        return pltpu.make_async_remote_copy(
-            src_ref=sent.at[n],
-            dst_ref=landed.at[n],
-            send_sem=bulk_send.at[n],
-            recv_sem=bulk_recv.at[n],
-            device_id={"section": sec + 1, "replica": me},
-            device_id_type=MESH,
-        )
-
-    def coefficients():
-        return pltpu.make_async_remote_copy(
-            src_ref=coef.at[1],
-            dst_ref=moved_coef,
-            send_sem=coef_send,
-            recv_sem=coef_recv,
-            device_id={"section": sec + 1, "replica": me},
-            device_id_type=MESH,
-        )
-
-    multiply(1, every, False)
-    for n in range(halves):
-        sent[n] = y[:, n * TILE : (n + 1) * TILE].astype(BF16)
-
-        @pl.when(sec < sections - 1)
+    for g in range(halves):
+        multiply(1, everything, g * TILE, TILE)
+        for k in range(g * per, (g + 1) * per):
+            flat_sent[k] = y[:, k * LANES : (k + 1) * LANES].astype(BF16)
+
+        @pl.when(has_next)
         def _():
-            bulk(n).start()
-
-    gather_statistics(1)
+            for k in range(g * per, (g + 1) * per):
+                if k < chunks - 1:
+                    bulk(k).start()
+
     send_statistics(1)
     combine(1, 1)
 
-    @pl.when(sec < sections - 1)
+    @pl.when(has_next)
     def _():
         coefficients().start()
+        bulk(chunks - 1).start()
 
     give_result(0, 1)
 
@@ -279,46 +303,57 @@
     def _():
         lay_maps(1)
 
-    def lay_landed(half):
-        bulk(half).wait_recv()
-        table = moved_coef[...]
-        for k in range(half * TILE // LANES, (half + 1) * TILE // LANES):
-            at = k * LANES - half * TILE
-            values = landed[half, :, at : at + LANES].astype(F32)
-            lay(k, activate(values, table, k))
-
     for half in range(halves):
 
-        @pl.when(sec > 0)
+        @pl.when(has_previous)
         def _():
             if half == 0:
                 coefficients().wait_recv()
-            lay_landed(half)
-
-        multiply(0, [(dy, half) for dy in range(3)], half > 0)
-    gather_statistics(2)
+            for k in range(half * per, (half + 1) * per):
+                bulk(k).wait_recv()
+                lay(k, activate(flat_landed[k].astype(F32), moved_coef, k))
+
+        multiply(0, [half], add=half > 0)
     send_statistics(2)
     combine(2, 0)
     lay_hidden(2)
 
-    multiply(1, every, False)
-    gather_statistics(3)
+    multiply(1, everything)
     send_statistics(3)
     combine(3, 1)
     give_result(1, 3)
 
     for phase in range(4):
-        pltpu.make_async_copy(slots.at[phase], slots.at[phase], stat_send.at[phase]).wait()
-
-    @pl.when(sec < sections - 1)
+        here = slots.at[phase]
+        pltpu.make_async_copy(here, here, stat_send.at[phase]).wait()
+
+    @pl.when(has_next)
     def _():
-        for n in range(halves):
-            bulk(n).wait_send()
+        for k in range(chunks):
+            bulk(k).wait_send()
         coefficients().wait_send()
 
     for copies in out_copies:
         for copy in copies:
             copy.wait()
+
+
+def hand_over(given, out, held, in_sems, out_sems):
+    ticks, rows = given.shape[1:3]
+    cut = (rows + 1) // 2
+    parts = [(t, p) for t in range(ticks) for p in (pl.ds(0, cut), pl.ds(cut, rows - cut))]
+    fetch, give = [], []
+    for n, (t, part) in enumerate(parts):
+        here = held.at[t, part]
+        fetch.append(pltpu.make_async_copy(given.at[0, t, part], here, in_sems.at[n]))
+        give.append(pltpu.make_async_copy(here, out.at[0, t, part], out_sems.at[n]))
+    for copy in fetch:
+        copy.start()
+    for one, other in zip(fetch, give):
+        one.wait()
+        other.start()
+    for copy in give:
+        copy.wait()
 
 
 def solution(mesh):
@@ -331,7 +366,8 @@
         pitch = SLOTS * images
         chunks = channels // LANES
         halves = channels // TILE
-        tile = 2 * channels // LANES
+        tile = 2 * chunks
+        limit = 56 * 2**20
         dma = pltpu.SemaphoreType.DMA
         anywhere = pl.BlockSpec(memory_space=pl.ANY)
         vmem = pl.BlockSpec(memory_space=pltpu.VMEM)
@@ -346,8 +382,8 @@
                 pltpu.VMEM((2, 3, 3, channels, channels), BF16),
                 pltpu.VMEM((halves, (rows + 2) * pitch, 3 * TILE), BF16),
                 pltpu.VMEM((rows * pitch, channels), F32),
-                pltpu.VMEM((halves, rows * pitch, TILE), BF16),
-                pltpu.VMEM((halves, rows * pitch, TILE), BF16),
+                pltpu.VMEM((chunks, rows, SLOTS, images, LANES), BF16),
+                pltpu.VMEM((chunks, rows, SLOTS, images, LANES), BF16),
                 pltpu.VMEM((4, tile, LANES), F32),
                 pltpu.VMEM((4, replicas - 1, tile, LANES), F32),
                 pltpu.VMEM((4, tile, LANES), F32),
@@ -359,13 +395,13 @@
                 dma((2, chunks)),
                 dma((4,)),
                 dma((4,)),
-                dma((halves,)),
-                dma((halves,)),
+                dma((chunks,)),
+                dma((chunks,)),
                 dma,
                 dma,
             ],
             compiler_params=pltpu.CompilerParams(
-                collective_id=0, has_side_effects=True, vmem_limit_bytes=56 * 2**20
+                collective_id=0, has_side_effects=True, vmem_limit_bytes=limit
             ),
             cost_estimate=pl.CostEstimate(
                 flops=8 * images * rows * cols * depth,
@@ -374,6 +410,15 @@
             ),
             name="relay",
         )(pend, arriving, first, second, gain, bias)
+        produced = pl.pallas_call(
+            hand_over,
+            out_shape=jax.ShapeDtypeStruct(produced.shape, BF16),
+            in_specs=[anywhere],
+            out_specs=anywhere,
+            scratch_shapes=[pltpu.VMEM(produced.shape[1:], BF16), dma((4,)), dma((4,))],
+            compiler_params=pltpu.CompilerParams(vmem_limit_bytes=limit),
+            name="hand_over",
+        )(produced)
         return jnp.transpose(produced, (0, 1, 4, 2, 3, 5))
 
     in_specs = (

time: 43.1 us -> 43.1 us (level)
  Pallas kernels: 40.3 us -> 42.9 us
  local copies, waits for them, and re-layouts: 2.58 us -> 0 us
    unnamed x1 -> x0, local copies, waits for them, and re-layouts: 2.58 us -> none
    pallas_call x0 -> x1, Pallas kernels: none -> 1.97 us  [body(): pl.pallas_call(hand_over, out_shape=jax.ShapeDtypeStruct(produced.shape,...]
    pallas_call x1, Pallas kernels: 40.3 us -> 40.9 us  [body(): pl.pallas_call(functools.partial(kernel, sections, replicas), out_shape=j...]
where the time goes in v4:
time: 43.1 us; the launch traced here: 42.9 us
  Pallas kernels  42.9 us (100%)
    pallas_call x1, Pallas kernels, body(): pl.pallas_call(functools.partial(kernel, sections, replicas), out_shape=j...  40.9 us
    pallas_call x1, Pallas kernels, body(): pl.pallas_call(hand_over, out_shape=jax.ShapeDtypeStruct(produced.shape,...  1.97 us

profile of v4, /device:TPU:3, one launch (start us, length us, event | category | flops | bytes accessed | tf_op | source)
XLA Modules:
  0.0 42.9 jit_solution(370996560061601671)
XLA Ops:
  0.0 40.9 %relay.1.given = bf16[1,2,14,14,2,512]{5,4,3,2,1,0:T(2,128)(2,1)} custom-call(bf16[1,14,14,2,512]{4,3,2,1,0:T(2,128)(2,1)} %bitcast.3, bf16[1,14,14,2,512]{4,3,2,1,0:T(2,128)(2,1)} %bitcast.4, bf16[1,3,3,512,512]{4,3,2,1,0:T(8,128)(2,1)} %first.1, bf16[1,3,3,512,512]{4,3,2,1,0:T(8,128)(2,1)} %second.1, f32[1,2,512]{2,1,0:T(2,128)} %gain.1, f32[1,2,512]{2,1,0:T(2,128)} %bias.1), custom_call_target="tpu_custom_call" | custom-call | flops 7398752256 | bytes 9437184 | tf_op jit(solution)/shard_map/relay/pallas_call | solution.py:375
  40.9 2.0 %hand_over.1 = bf16[1,2,14,14,2,512]{5,4,3,2,1,0:T(2,128)(2,1)} custom-call(bf16[1,2,14,14,2,512]{5,4,3,2,1,0:T(2,128)(2,1)} %relay.1.given), custom_call_target="tpu_custom_call" | custom-call | tf_op jit(solution)/shard_map/hand_over/pallas_call | solution.py:413

commit v5 on v4

--- a/solution.py
+++ b/solution.py
@@ -81,10 +81,11 @@
         )
 
     def lanes(k):
-        return pl.ds(pl.multiple_of(k * LANES, LANES), LANES)
+        return slice(k * LANES, (k + 1) * LANES)
 
     def each(count, step):
-        lax.fori_loop(0, count, lambda i, carry: step(i), None)
+        for i in range(count):
+            step(i)
 
     map_copies = [
         [
@@ -147,41 +148,38 @@
         half, lane = k // per, (k % per) * LANES
         shifted = (pltpu.roll(flat, images, 0), flat, pltpu.roll(flat, rows * pitch - images, 0))
         for dx, tap in enumerate(shifted):
-            at = pl.multiple_of(dx * TILE + lane, LANES)
-            taps[half, pitch : (rows + 1) * pitch, pl.ds(at, LANES)] = tap.astype(BF16)
+            at = dx * TILE + lane
+            taps[half, pitch : (rows + 1) * pitch, at : at + LANES] = tap.astype(BF16)
 
     def lay_maps(which):
         each(chunks, lambda k: lay(k, flat_maps[which, k].astype(F32)))
 
-    def product(layer, dy, half, lane, width):
-        left = taps[half, pl.ds(pl.multiple_of(dy * pitch, pitch), rows * pitch), :]
-        right = weights[layer, dy, :, half * TILE : (half + 1) * TILE, lane : lane + width]
-        return jnp.dot(left, right.reshape(3 * TILE, width), preferred_element_type=F32)
-
-    def multiply(layer, parts, lane=0, width=channels, add=False, ready=None):
+    def multiply(layer, parts, lane=0, width=channels, add=False):
+        left = jnp.concatenate(
+            [taps[half, dy * pitch : (dy + rows) * pitch, :] for dy, half in parts], axis=1
+        )
+        right = jnp.concatenate(
+            [
+                weights[layer, dy, :, half * TILE : (half + 1) * TILE, lane : lane + width].reshape(
+                    3 * TILE, width
+                )
+                for dy, half in parts
+            ],
+            axis=0,
+        )
+        total = jnp.dot(left, right, preferred_element_type=F32)
         where = slice(lane, lane + width)
-        if not add:
-            y[:, where] = jnp.zeros((rows * pitch, width), F32)
-
-        def step(dy):
-            if ready is not None:
-                ready(dy)
-            total = y[:, where]
-            for half in parts:
-                total = total + product(layer, dy, half, lane, width)
-            y[:, where] = total
-
-        each(3, step)
-
-    everything = range(halves)
+        y[:, where] = y[:, where] + total if add else total
+
+    everything = [(dy, half) for half in range(halves) for dy in range(3)]
 
     def send_statistics(phase):
         def measure(k):
             total = jnp.sum(jnp.where(inside, y[:, lanes(k)], 0.0), axis=0, keepdims=True)
             mean = total / cells
             centred = jnp.where(inside, y[:, lanes(k)] - mean, 0.0)
-            mine[phase, pl.ds(k, 1), :] = mean
-            mine[phase, pl.ds(chunks + k, 1), :] = jnp.sum(
+            mine[phase, k : k + 1, :] = mean
+            mine[phase, chunks + k : chunks + k + 1, :] = jnp.sum(
                 centred * centred, axis=0, keepdims=True
             )
 
@@ -222,8 +220,8 @@
         coef[phase, chunks:, :] = affine[layer, chunks:, :] - mean * scale
 
     def activate(values, table, k):
-        scale = table[pl.ds(k, 1), :]
-        offset = table[pl.ds(chunks + k, 1), :]
+        scale = table[k : k + 1, :]
+        offset = table[chunks + k : chunks + k + 1, :]
         return jnp.maximum(values * scale + offset, 0.0)
 
     def lay_hidden(phase):
@@ -263,13 +261,9 @@
     for copy in map_copies[0]:
         copy.wait()
     lay_maps(0)
-    multiply(
-        0,
-        everything,
-        ready=lambda dy: pltpu.make_async_copy(
-            first.at[0, dy], weights.at[0, dy], weight_sem.at[0, dy]
-        ).wait(),
-    )
+    for dy in range(3):
+        weight_copies[0][dy].wait()
+        multiply(0, [(dy, half) for half in range(halves)], add=dy > 0)
     send_statistics(0)
     for dy in range(3):
         weight_copies[1][dy].wait()
@@ -313,7 +307,7 @@
                 bulk(k).wait_recv()
                 lay(k, activate(flat_landed[k].astype(F32), moved_coef, k))
 
-        multiply(0, [half], add=half > 0)
+        multiply(0, [(dy, half) for dy in range(3)], add=half > 0)
     send_statistics(2)
     combine(2, 0)
     lay_hidden(2)

time: 43.1 us -> 40.3 us (0.935)
  Pallas kernels: 42.9 us -> 40.1 us
    pallas_call x1, Pallas kernels: 40.9 us -> 38.1 us  [body(): pl.pallas_call(functools.partial(kernel, sections, replicas), out_shape=j...]
where the time goes in v5:
time: 40.3 us; the launch traced here: 40.1 us
  Pallas kernels  40.1 us (100%)
    pallas_call x1, Pallas kernels, body(): pl.pallas_call(functools.partial(kernel, sections, replicas), out_shape=j...  38.1 us
    pallas_call x1, Pallas kernels, body(): pl.pallas_call(hand_over, out_shape=jax.ShapeDtypeStruct(produced.shape,...  1.97 us

profile of v5, /device:TPU:3, one launch (start us, length us, event | category | flops | bytes accessed | tf_op | source)
XLA Modules:
  0.0 40.1 jit_solution(2152164852792818595)
XLA Ops:
  0.0 38.1 %relay.1.given = bf16[1,2,14,14,2,512]{5,4,3,2,1,0:T(2,128)(2,1)} custom-call(bf16[1,14,14,2,512]{4,3,2,1,0:T(2,128)(2,1)} %bitcast.3, bf16[1,14,14,2,512]{4,3,2,1,0:T(2,128)(2,1)} %bitcast.4, bf16[1,3,3,512,512]{4,3,2,1,0:T(8,128)(2,1)} %first.1, bf16[1,3,3,512,512]{4,3,2,1,0:T(8,128)(2,1)} %second.1, f32[1,2,512]{2,1,0:T(2,128)} %gain.1, f32[1,2,512]{2,1,0:T(2,128)} %bias.1), custom_call_target="tpu_custom_call" | custom-call | flops 7398752256 | bytes 9437184 | tf_op jit(solution)/shard_map/relay/pallas_call | solution.py:369
  38.1 2.0 %hand_over.1 = bf16[1,2,14,14,2,512]{5,4,3,2,1,0:T(2,128)(2,1)} custom-call(bf16[1,2,14,14,2,512]{5,4,3,2,1,0:T(2,128)(2,1)} %relay.1.given), custom_call_target="tpu_custom_call" | custom-call | tf_op jit(solution)/shard_map/hand_over/pallas_call | solution.py:407

commit v6 on v5

--- a/solution.py
+++ b/solution.py
@@ -155,19 +155,12 @@
         each(chunks, lambda k: lay(k, flat_maps[which, k].astype(F32)))
 
     def multiply(layer, parts, lane=0, width=channels, add=False):
-        left = jnp.concatenate(
-            [taps[half, dy * pitch : (dy + rows) * pitch, :] for dy, half in parts], axis=1
-        )
-        right = jnp.concatenate(
-            [
-                weights[layer, dy, :, half * TILE : (half + 1) * TILE, lane : lane + width].reshape(
-                    3 * TILE, width
-                )
-                for dy, half in parts
-            ],
-            axis=0,
-        )
-        total = jnp.dot(left, right, preferred_element_type=F32)
+        total = None
+        for dy, half in parts:
+            left = taps[half, dy * pitch : (dy + rows) * pitch, :]
+            right = weights[layer, dy, :, half * TILE : (half + 1) * TILE, lane : lane + width]
+            term = jnp.dot(left, right.reshape(3 * TILE, width), preferred_element_type=F32)
+            total = term if total is None else total + term
         where = slice(lane, lane + width)
         y[:, where] = y[:, where] + total if add else total
 

time: 40.3 us -> 40.3 us (level)
  no operation moved by 1% of the time
where the time goes in v6:
time: 40.3 us; the launch traced here: 40.1 us
  Pallas kernels  40.1 us (100%)
    pallas_call x1, Pallas kernels, body(): pl.pallas_call(functools.partial(kernel, sections, replicas), out_shape=j...  38.1 us
    pallas_call x1, Pallas kernels, body(): pl.pallas_call(hand_over, out_shape=jax.ShapeDtypeStruct(produced.shape,...  1.97 us

profile of v6, /device:TPU:3, one launch (start us, length us, event | category | flops | bytes accessed | tf_op | source)
XLA Modules:
  0.0 40.1 jit_solution(6747879283586921586)
XLA Ops:
  0.0 38.1 %relay.1.given = bf16[1,2,14,14,2,512]{5,4,3,2,1,0:T(2,128)(2,1)} custom-call(bf16[1,14,14,2,512]{4,3,2,1,0:T(2,128)(2,1)} %bitcast.3, bf16[1,14,14,2,512]{4,3,2,1,0:T(2,128)(2,1)} %bitcast.4, bf16[1,3,3,512,512]{4,3,2,1,0:T(8,128)(2,1)} %first.1, bf16[1,3,3,512,512]{4,3,2,1,0:T(8,128)(2,1)} %second.1, f32[1,2,512]{2,1,0:T(2,128)} %gain.1, f32[1,2,512]{2,1,0:T(2,128)} %bias.1), custom_call_target="tpu_custom_call" | custom-call | flops 7398752256 | bytes 9437184 | tf_op jit(solution)/shard_map/relay/pallas_call | solution.py:362
  38.1 2.0 %hand_over.1 = bf16[1,2,14,14,2,512]{5,4,3,2,1,0:T(2,128)(2,1)} custom-call(bf16[1,2,14,14,2,512]{5,4,3,2,1,0:T(2,128)(2,1)} %relay.1.given), custom_call_target="tpu_custom_call" | custom-call | tf_op jit(solution)/shard_map/hand_over/pallas_call | solution.py:400

commit v7 on v6

--- a/solution.py
+++ b/solution.py
@@ -265,16 +265,14 @@
     combine(0, 0)
     lay_hidden(0)
 
-    for g in range(halves):
-        multiply(1, everything, g * TILE, TILE)
-        for k in range(g * per, (g + 1) * per):
-            flat_sent[k] = y[:, k * LANES : (k + 1) * LANES].astype(BF16)
+    multiply(1, everything)
+    for k in range(chunks):
+        flat_sent[k] = y[:, k * LANES : (k + 1) * LANES].astype(BF16)
 
         @pl.when(has_next)
         def _():
-            for k in range(g * per, (g + 1) * per):
-                if k < chunks - 1:
-                    bulk(k).start()
+            if k < chunks - 1:
+                bulk(k).start()
 
     send_statistics(1)
     combine(1, 1)

time: 40.3 us -> 40.3 us (level)
  no operation moved by 1% of the time
where the time goes in v7:
time: 40.3 us; the launch traced here: 40.1 us
  Pallas kernels  40.1 us (100%)
    pallas_call x1, Pallas kernels, body(): pl.pallas_call(functools.partial(kernel, sections, replicas), out_shape=j...  38.1 us
    pallas_call x1, Pallas kernels, body(): pl.pallas_call(hand_over, out_shape=jax.ShapeDtypeStruct(produced.shape,...  1.97 us

profile of v7, /device:TPU:3, one launch (start us, length us, event | category | flops | bytes accessed | tf_op | source)
XLA Modules:
  0.0 40.1 jit_solution(6612909756511627639)
XLA Ops:
  0.0 38.1 %relay.1.given = bf16[1,2,14,14,2,512]{5,4,3,2,1,0:T(2,128)(2,1)} custom-call(bf16[1,14,14,2,512]{4,3,2,1,0:T(2,128)(2,1)} %bitcast.3, bf16[1,14,14,2,512]{4,3,2,1,0:T(2,128)(2,1)} %bitcast.4, bf16[1,3,3,512,512]{4,3,2,1,0:T(8,128)(2,1)} %first.1, bf16[1,3,3,512,512]{4,3,2,1,0:T(8,128)(2,1)} %second.1, f32[1,2,512]{2,1,0:T(2,128)} %gain.1, f32[1,2,512]{2,1,0:T(2,128)} %bias.1), custom_call_target="tpu_custom_call" | custom-call | flops 7398752256 | bytes 9437184 | tf_op jit(solution)/shard_map/relay/pallas_call | solution.py:360
  38.1 2.0 %hand_over.1 = bf16[1,2,14,14,2,512]{5,4,3,2,1,0:T(2,128)(2,1)} custom-call(bf16[1,2,14,14,2,512]{5,4,3,2,1,0:T(2,128)(2,1)} %relay.1.given), custom_call_target="tpu_custom_call" | custom-call | tf_op jit(solution)/shard_map/hand_over/pallas_call | solution.py:398
